TPU v7x, 32 devices: a whole 2x2x4 slice. The times are simulated.
32 devices in a mesh: ingest: 8 (over y, x, core), section: 4 (over z).
Axes of the slice: x: 2, y: 2, z: 4, core: 2. Of those that a mesh axis runs over, the one named last changes fastest.
Arguments:
- txn_feats: bfloat16 [8192, 2048], P(('ingest', 'section')), may hold values from -6 to 6
- txn_seg: int32 [32, 256], P(('ingest', 'section')), may hold values from 0 to 63, as said below
- seg_row: int32 [32, 64], P(('ingest', 'section')), may hold values from 0 to 15, as said below
- send_counts: int32 [32, 8], P(('ingest', 'section')), may hold values from 0 to 8, as said below
- gains: float32 [4, 2048], P('section'), may hold values from 0.5 to 1.5
- tower_w: bfloat16 [4, 2048, 2048], P('section', 'ingest'), may hold values from -0.125 to 0.125
Outputs:
- card_embed: bfloat16 [512, 2048], P(('ingest', 'section'))
Inputs may be any that keep to these rules, and one draw needn't show every extreme that they name: Each row of send_counts is at most 8 everywhere; in each section index one owner index gets exactly 8 from every device of that section; device 0 sends exactly 8 to every owner. Within a device's row txn_seg never falls, starts at 0 and ends at that device's sum of send_counts minus one. `seg_row`: the segments that one device sends to one owner name different card rows.
All inputs are finite; a program needn't handle non-finite values.
Results may differ from a plain program's by a relative error of at most 0.012.
Values may be sent and summed in bfloat16 or wider, within the bound.
A program may use at most 64 MiB of HBM per device.

v0:
```python
import jax
import jax.numpy as jnp
from jax import lax
from jax.sharding import PartitionSpec as P

CARD_DEV = 16


def from_behind(x, axis, by):
    count = lax.axis_size(axis)
    pairs = [(i, i + by) for i in range(count) if 0 <= i + by < count]
    return lax.ppermute(x, axis, pairs)


def broadcast(x, axis, root):
    mine = lax.axis_index(axis) == root
    return lax.psum(jnp.where(mine, x, jnp.zeros_like(x)), axis)


def tower_layer(x, gain, weight):
    u = x.astype(jnp.float32)
    mean_sq = jnp.mean(u * u, axis=-1, keepdims=True)
    normed = (u * lax.rsqrt(mean_sq + 1e-05) * gain).astype(jnp.bfloat16)
    y = jnp.dot(normed, weight, preferred_element_type=jnp.float32)
    return (u + jax.nn.silu(y)).astype(jnp.bfloat16)


def body(txn_feats, txn_seg, seg_row, send_counts, gains, tower_w):
    width = txn_feats.shape[1]
    owners = lax.axis_size("ingest")
    sections = lax.axis_size("section")
    slots = seg_row.shape[1]
    cards = CARD_DEV
    weight = lax.all_gather(tower_w[0], "ingest", axis=0, tiled=True)
    gain = gains[0]
    counts = send_counts[0]
    ends = jnp.cumsum(counts)
    seg = txn_seg[0]
    rows = seg_row[0]
    slot_ids = jnp.arange(slots, dtype=jnp.int32)
    txn_owner = jnp.sum((seg[:, None] >= ends[None, :]).astype(jnp.int32), axis=1)
    txn_row = jnp.sum((seg[:, None] == slot_ids[None, :]).astype(jnp.int32) * rows[None, :], axis=1)
    target = txn_owner * cards + txn_row
    place = (jnp.arange(owners * cards, dtype=jnp.int32)[:, None] == target[None, :]).astype(
        jnp.bfloat16
    )
    buffer = jnp.dot(place, txn_feats, preferred_element_type=jnp.float32).astype(jnp.bfloat16)
    buffer = buffer.reshape(owners, cards, width)
    received = lax.all_to_all(buffer, "ingest", split_axis=0, concat_axis=0, tiled=True)
    pooled = jnp.sum(received, axis=0, dtype=jnp.float32).astype(jnp.bfloat16)
    section_pos = lax.axis_index("section")
    total_steps = 2 * sections - 1
    blocks = lax.all_gather(pooled[None], "section", axis=0, tiled=True)

    def advance(step, carry):
        current, finished, waiting = carry
        incoming = from_behind(current, "section", 1)
        fresh = lax.dynamic_index_in_dim(blocks, jnp.minimum(step, sections - 1), 0, keepdims=False)
        entry = jnp.where(section_pos == 0, fresh, incoming)
        active = (step >= section_pos) & (step < section_pos + sections)
        result = lax.cond(active, lambda v: tower_layer(v, gain, weight), lambda v: v, entry)
        place_at = jnp.clip(step - (sections - 1), 0, sections - 1)
        keep = (section_pos == sections - 1) & (step >= sections - 1)
        before = lax.dynamic_index_in_dim(finished, place_at, 0, keepdims=False)
        finished = lax.dynamic_update_index_in_dim(
            finished, jnp.where(keep, result, before), place_at, 0
        )
        return (result, finished, waiting)

    start_state = (
        jnp.zeros_like(pooled),
        jnp.zeros((sections, cards, width), jnp.bfloat16),
        pooled,
    )
    final_state = lax.fori_loop(0, total_steps, advance, start_state)
    everything = broadcast(final_state[1], "section", sections - 1)
    return lax.dynamic_index_in_dim(everything, section_pos, 0, keepdims=False)


def solution(mesh):
    in_specs = (
        P(("ingest", "section"), None),
        P(("ingest", "section"), None),
        P(("ingest", "section"), None),
        P(("ingest", "section"), None),
        P("section", None),
        P("section", "ingest", None),
    )
    out_specs = P(("ingest", "section"), None)
    return jax.shard_map(body, mesh=mesh, in_specs=in_specs, out_specs=out_specs, check_vma=False)
```

profile of v0, /device:TPU:0, one launch (start us, length us, event | category | flops | bytes accessed | tf_op | source)
XLA Modules:
  0.0 184.6 jit_solution(12346216078451235572)
XLA Ops:
  6.5 0.0 copy-start
  6.5 0.0 all-gather.4.cloned.1.call-start
  6.5 0.7 all-gather.4.cloned.1.call-update
  7.3 0.8 reduce-window.8
  8.1 0.8 convert_reduce_fusion
  8.9 0.8 select_reduce_fusion
  9.6 0.0 copy-done
  9.7 1.2 convolution_convert_fusion
  10.8 5.2 %all-to-all-start = ((bf16[8,16,2048]{2,1,0:T(8,128)(2,1)}), bf16[8,16,2048]{2,1,0:T(8,128)(2,1)S(1)}, u32[]{:S(2)}, u32[]{:S(2)}) async-start(bf16[8,16,2048]{2,1,0:T(8,128)(2,1)} %bitcast.8), calls=%async_computation | async-start | bytes 1048576 | tf_op jit(solution)/shard_map/all_to_all | solution.py:49
  16.0 0.0 all-reduce.2.cloned.1.call-start
  16.0 12.4 %all-to-all-done = bf16[8,16,2048]{2,1,0:T(8,128)(2,1)S(1)} async-done(((bf16[8,16,2048]{2,1,0:T(8,128)(2,1)}), bf16[8,16,2048]{2,1,0:T(8,128)(2,1)S(1)}, u32[]{:S(2)}, u32[]{:S(2)}) %all-to-all-start) | async-done | bytes 524320 | tf_op jit(solution)/shard_map/all_to_all | solution.py:49
  28.4 0.1 reduce_sum.41
  28.5 14.7 %all-gather = bf16[64,2048]{1,0:T(8,128)(2,1)S(1)} all-gather(bf16[16,2048]{1,0:T(8,128)(2,1)S(1)} %reduce_sum.41), channel_id=2, replica_groups=mesh['ingest'=8,'section'=4] {'section'}, dimensions={0}, use_global_device_ids=true | all-gather | bytes 327680 | tf_op jit(solution)/shard_map/all_gather | solution.py:53
  43.2 25.3 %all-gather.4.cloned.1.call-done = bf16[1,2048,2048]{2,1,0:T(8,128)(2,1)} async-done(((bf16[1,256,2048]{2,1,0:T(8,128)(2,1)}), bf16[1,2048,2048]{2,1,0:T(8,128)(2,1)}) %all-gather.4.cloned.1.call-update) | async-done | bytes 8388624 | tf_op jit(solution)/shard_map/all_gather | solution.py:34
  68.5 63.9 %while.17 = (s32[]{:T(128)}, bf16[16,2048]{1,0:T(8,128)(2,1)S(1)}, bf16[4,16,2048]{2,1,0:T(8,128)(2,1)S(1)}, s32[]{:T(128)}, s32[]{:T(128)}, /*index=5*/pred[]{:...) while((s32[]{:T(128)}, bf16[16,2048]{1,0:T(8,128)(2,1)S(1)}, ...), condition=%wide.region_8.9_spmd, body=%wide.region_4.8_spmd.sunk | while | flops 134742048 | bytes 9511515 | solution.py:75
  68.6 3.4 %collective-permute-start = (bf16[16,2048]{1,0:T(8,128)(2,1)S(1)}, bf16[16,2048]{1,0:T(8,128)(2,1)S(1)}, u32[]{:S(2)}, u32[]{:S(2)}) collective-permute-start(bf16[16,2048]{1,0:T(8,128)(2,1)S(1)} %get-tuple-element.315), channel_id=1, source_target_pairs={{0,1},{1,2},{2,3},{4,5},{5,6},{6,7},{8,9},{9,10},{10,11},{12,13},{... | collective-permute-start | bytes 196616 | tf_op jit(solution)/shard_map/while/body/eval_jaxpr/ppermute | solution.py:12
  72.0 1.8 collective-permute-done
  73.9 4.8 %conditional.2 = (bf16[16,2048]{1,0:T(8,128)(2,1)S(1)}) conditional(s32[]{:T(128)} %convert_element_type.53, bf16[16,2048]{1,0:T(8,128)(2,1)S(1)} %bitcast_select_fusion.3, (bf16[16,2048]{1,0:T(8,128)(2,1)S(1)}, f32[1,2048]{1,0:T(1,128)}, bf16[2048,2048]{1,0:T(8,128)(2,1)}) %tuple.50), branch_computations={%region_5.5_spmd, %region_6.7_spmd} | conditional | flops 134676496 | bytes 8724744 | solution.py:61
  73.9 0.1 fusion
  74.0 4.7 %fusion.3 = bf16[16,2048]{1,0:T(8,128)(2,1)S(1)} fusion(bf16[16,2048]{1,0:T(8,128)(2,1)S(1)} %copy.20, bf16[2048,2048]{1,0:T(8,128)(2,1)} %get-tuple-element.204, f32[2048]{0:T(1024)} %bitcast.27, f32[16]{0:T(128)S(1)} %add_rsqrt_fusion), kind=kOutput, calls=%fused_computation.6 | convolution fusion | flops 134578176 | bytes 8527936 | tf_op jit(solution)/shard_map/while/body/eval_jaxpr/cond/branch_1_fun/dot_general | solution.py:24
  78.7 1.3 collective-permute-start
  80.1 1.8 collective-permute-done
  81.9 4.8 %conditional.2 = (bf16[16,2048]{1,0:T(8,128)(2,1)S(1)}) conditional(s32[]{:T(128)} %convert_element_type.53, bf16[16,2048]{1,0:T(8,128)(2,1)S(1)} %bitcast_select_fusion.3, (bf16[16,2048]{1,0:T(8,128)(2,1)S(1)}, f32[1,2048]{1,0:T(1,128)}, bf16[2048,2048]{1,0:T(8,128)(2,1)}) %tuple.50), branch_computations={%region_5.5_spmd, %region_6.7_spmd} | conditional | flops 134676496 | bytes 8724744 | solution.py:61
  82.0 0.1 fusion
  82.1 4.7 %fusion.3 = bf16[16,2048]{1,0:T(8,128)(2,1)S(1)} fusion(bf16[16,2048]{1,0:T(8,128)(2,1)S(1)} %copy.20, bf16[2048,2048]{1,0:T(8,128)(2,1)} %get-tuple-element.204, f32[2048]{0:T(1024)} %bitcast.27, f32[16]{0:T(128)S(1)} %add_rsqrt_fusion), kind=kOutput, calls=%fused_computation.6 | convolution fusion | flops 134578176 | bytes 8527936 | tf_op jit(solution)/shard_map/while/body/eval_jaxpr/cond/branch_1_fun/dot_general | solution.py:24
  86.8 4.3 %collective-permute-start = (bf16[16,2048]{1,0:T(8,128)(2,1)S(1)}, bf16[16,2048]{1,0:T(8,128)(2,1)S(1)}, u32[]{:S(2)}, u32[]{:S(2)}) collective-permute-start(bf16[16,2048]{1,0:T(8,128)(2,1)S(1)} %get-tuple-element.315), channel_id=1, source_target_pairs={{0,1},{1,2},{2,3},{4,5},{5,6},{6,7},{8,9},{9,10},{10,11},{12,13},{... | collective-permute-start | bytes 196616 | tf_op jit(solution)/shard_map/while/body/eval_jaxpr/ppermute | solution.py:12
  91.1 1.8 collective-permute-done
  93.0 4.8 %conditional.2 = (bf16[16,2048]{1,0:T(8,128)(2,1)S(1)}) conditional(s32[]{:T(128)} %convert_element_type.53, bf16[16,2048]{1,0:T(8,128)(2,1)S(1)} %bitcast_select_fusion.3, (bf16[16,2048]{1,0:T(8,128)(2,1)S(1)}, f32[1,2048]{1,0:T(1,128)}, bf16[2048,2048]{1,0:T(8,128)(2,1)}) %tuple.50), branch_computations={%region_5.5_spmd, %region_6.7_spmd} | conditional | flops 134676496 | bytes 8724744 | solution.py:61
  93.0 0.1 fusion
  93.2 4.7 %fusion.3 = bf16[16,2048]{1,0:T(8,128)(2,1)S(1)} fusion(bf16[16,2048]{1,0:T(8,128)(2,1)S(1)} %copy.20, bf16[2048,2048]{1,0:T(8,128)(2,1)} %get-tuple-element.204, f32[2048]{0:T(1024)} %bitcast.27, f32[16]{0:T(128)S(1)} %add_rsqrt_fusion), kind=kOutput, calls=%fused_computation.6 | convolution fusion | flops 134578176 | bytes 8527936 | tf_op jit(solution)/shard_map/while/body/eval_jaxpr/cond/branch_1_fun/dot_general | solution.py:24
  97.9 4.3 %collective-permute-start = (bf16[16,2048]{1,0:T(8,128)(2,1)S(1)}, bf16[16,2048]{1,0:T(8,128)(2,1)S(1)}, u32[]{:S(2)}, u32[]{:S(2)}) collective-permute-start(bf16[16,2048]{1,0:T(8,128)(2,1)S(1)} %get-tuple-element.315), channel_id=1, source_target_pairs={{0,1},{1,2},{2,3},{4,5},{5,6},{6,7},{8,9},{9,10},{10,11},{12,13},{... | collective-permute-start | bytes 196616 | tf_op jit(solution)/shard_map/while/body/eval_jaxpr/ppermute | solution.py:12
  102.2 1.8 collective-permute-done
  104.0 4.8 %conditional.2 = (bf16[16,2048]{1,0:T(8,128)(2,1)S(1)}) conditional(s32[]{:T(128)} %convert_element_type.53, bf16[16,2048]{1,0:T(8,128)(2,1)S(1)} %bitcast_select_fusion.3, (bf16[16,2048]{1,0:T(8,128)(2,1)S(1)}, f32[1,2048]{1,0:T(1,128)}, bf16[2048,2048]{1,0:T(8,128)(2,1)}) %tuple.50), branch_computations={%region_5.5_spmd, %region_6.7_spmd} | conditional | flops 134676496 | bytes 8724744 | solution.py:61
  104.1 0.1 fusion
  104.2 4.7 %fusion.3 = bf16[16,2048]{1,0:T(8,128)(2,1)S(1)} fusion(bf16[16,2048]{1,0:T(8,128)(2,1)S(1)} %copy.20, bf16[2048,2048]{1,0:T(8,128)(2,1)} %get-tuple-element.204, f32[2048]{0:T(1024)} %bitcast.27, f32[16]{0:T(128)S(1)} %add_rsqrt_fusion), kind=kOutput, calls=%fused_computation.6 | convolution fusion | flops 134578176 | bytes 8527936 | tf_op jit(solution)/shard_map/while/body/eval_jaxpr/cond/branch_1_fun/dot_general | solution.py:24
  108.9 4.3 %collective-permute-start = (bf16[16,2048]{1,0:T(8,128)(2,1)S(1)}, bf16[16,2048]{1,0:T(8,128)(2,1)S(1)}, u32[]{:S(2)}, u32[]{:S(2)}) collective-permute-start(bf16[16,2048]{1,0:T(8,128)(2,1)S(1)} %get-tuple-element.315), channel_id=1, source_target_pairs={{0,1},{1,2},{2,3},{4,5},{5,6},{6,7},{8,9},{9,10},{10,11},{12,13},{... | collective-permute-start | bytes 196616 | tf_op jit(solution)/shard_map/while/body/eval_jaxpr/ppermute | solution.py:12
  113.3 1.8 collective-permute-done
  115.2 9.1 %collective-permute-start = (bf16[16,2048]{1,0:T(8,128)(2,1)S(1)}, bf16[16,2048]{1,0:T(8,128)(2,1)S(1)}, u32[]{:S(2)}, u32[]{:S(2)}) collective-permute-start(bf16[16,2048]{1,0:T(8,128)(2,1)S(1)} %get-tuple-element.315), channel_id=1, source_target_pairs={{0,1},{1,2},{2,3},{4,5},{5,6},{6,7},{8,9},{9,10},{10,11},{12,13},{... | collective-permute-start | bytes 196616 | tf_op jit(solution)/shard_map/while/body/eval_jaxpr/ppermute | solution.py:12
  124.3 1.8 collective-permute-done
  126.2 4.3 %collective-permute-start = (bf16[16,2048]{1,0:T(8,128)(2,1)S(1)}, bf16[16,2048]{1,0:T(8,128)(2,1)S(1)}, u32[]{:S(2)}, u32[]{:S(2)}) collective-permute-start(bf16[16,2048]{1,0:T(8,128)(2,1)S(1)} %get-tuple-element.315), channel_id=1, source_target_pairs={{0,1},{1,2},{2,3},{4,5},{5,6},{6,7},{8,9},{9,10},{10,11},{12,13},{... | collective-permute-start | bytes 196616 | tf_op jit(solution)/shard_map/while/body/eval_jaxpr/ppermute | solution.py:12
  130.6 1.8 collective-permute-done
  132.5 0.7 broadcast_select_fusion
  133.2 0.0 all-reduce.2.cloned.1.call-update
  133.2 43.0 %all-reduce.2.cloned.1.call-done = bf16[4,16,2048]{2,1,0:T(8,128)(2,1)} async-done(((bf16[4,16,2048]{2,1,0:T(8,128)(2,1)}), bf16[4,16,2048]{2,1,0:T(8,128)(2,1)}) %all-reduce.2.cloned.1.call-update) | async-done | bytes 262160 | tf_op jit(solution)/shard_map/psum | solution.py:17
  176.2 1.5 dynamic-slice_bitcast_fusion
  (35 shorter events, 0.4 us)
Async XLA Ops:
  6.5 3.1 %copy-start = (bf16[256,2048]{1,0:T(8,128)(2,1)S(1)}, bf16[256,2048]{1,0:T(8,128)(2,1)}, u32[]{:S(2)}) copy-start(bf16[256,2048]{1,0:T(8,128)(2,1)} %param.10) | copy-start | bytes 3145732
  6.5 62.0 %all-gather.4.cloned.1.call-start = ((), (), s32[]{:S(2)}) async-start(), calls=%async_computation.2 | async-start | bytes 9437184 | tf_op jit(solution)/shard_map/all_gather | solution.py:34
  10.8 17.6 %all-to-all-start = ((bf16[8,16,2048]{2,1,0:T(8,128)(2,1)}), bf16[8,16,2048]{2,1,0:T(8,128)(2,1)S(1)}, u32[]{:S(2)}, u32[]{:S(2)}) async-start(bf16[8,16,2048]{2,1,0:T(8,128)(2,1)} %bitcast.8), calls=%async_computation | async-start | bytes 1048576 | tf_op jit(solution)/shard_map/all_to_all | solution.py:49
  16.0 160.3 %all-reduce.2.cloned.1.call-start = ((), (), s32[]{:S(2)}) async-start(), calls=%async_computation.1 | async-start | bytes 524288 | tf_op jit(solution)/shard_map/psum | solution.py:17
  68.6 5.3 %collective-permute-start = (bf16[16,2048]{1,0:T(8,128)(2,1)S(1)}, bf16[16,2048]{1,0:T(8,128)(2,1)S(1)}, u32[]{:S(2)}, u32[]{:S(2)}) collective-permute-start(bf16[16,2048]{1,0:T(8,128)(2,1)S(1)} %get-tuple-element.315), channel_id=1, source_target_pairs={{0,1},{1,2},{2,3},{4,5},{5,6},{6,7},{8,9},{9,10},{10,11},{12,13},{... | collective-permute-start | bytes 196616 | tf_op jit(solution)/shard_map/while/body/eval_jaxpr/ppermute | solution.py:12
  78.7 3.2 %collective-permute-start = (bf16[16,2048]{1,0:T(8,128)(2,1)S(1)}, bf16[16,2048]{1,0:T(8,128)(2,1)S(1)}, u32[]{:S(2)}, u32[]{:S(2)}) collective-permute-start(bf16[16,2048]{1,0:T(8,128)(2,1)S(1)} %get-tuple-element.315), channel_id=1, source_target_pairs={{0,1},{1,2},{2,3},{4,5},{5,6},{6,7},{8,9},{9,10},{10,11},{12,13},{... | collective-permute-start | bytes 196616 | tf_op jit(solution)/shard_map/while/body/eval_jaxpr/ppermute | solution.py:12
  86.8 6.2 %collective-permute-start = (bf16[16,2048]{1,0:T(8,128)(2,1)S(1)}, bf16[16,2048]{1,0:T(8,128)(2,1)S(1)}, u32[]{:S(2)}, u32[]{:S(2)}) collective-permute-start(bf16[16,2048]{1,0:T(8,128)(2,1)S(1)} %get-tuple-element.315), channel_id=1, source_target_pairs={{0,1},{1,2},{2,3},{4,5},{5,6},{6,7},{8,9},{9,10},{10,11},{12,13},{... | collective-permute-start | bytes 196616 | tf_op jit(solution)/shard_map/while/body/eval_jaxpr/ppermute | solution.py:12
  97.9 6.2 %collective-permute-start = (bf16[16,2048]{1,0:T(8,128)(2,1)S(1)}, bf16[16,2048]{1,0:T(8,128)(2,1)S(1)}, u32[]{:S(2)}, u32[]{:S(2)}) collective-permute-start(bf16[16,2048]{1,0:T(8,128)(2,1)S(1)} %get-tuple-element.315), channel_id=1, source_target_pairs={{0,1},{1,2},{2,3},{4,5},{5,6},{6,7},{8,9},{9,10},{10,11},{12,13},{... | collective-permute-start | bytes 196616 | tf_op jit(solution)/shard_map/while/body/eval_jaxpr/ppermute | solution.py:12
  108.9 6.2 %collective-permute-start = (bf16[16,2048]{1,0:T(8,128)(2,1)S(1)}, bf16[16,2048]{1,0:T(8,128)(2,1)S(1)}, u32[]{:S(2)}, u32[]{:S(2)}) collective-permute-start(bf16[16,2048]{1,0:T(8,128)(2,1)S(1)} %get-tuple-element.315), channel_id=1, source_target_pairs={{0,1},{1,2},{2,3},{4,5},{5,6},{6,7},{8,9},{9,10},{10,11},{12,13},{... | collective-permute-start | bytes 196616 | tf_op jit(solution)/shard_map/while/body/eval_jaxpr/ppermute | solution.py:12
  115.2 11.0 %collective-permute-start = (bf16[16,2048]{1,0:T(8,128)(2,1)S(1)}, bf16[16,2048]{1,0:T(8,128)(2,1)S(1)}, u32[]{:S(2)}, u32[]{:S(2)}) collective-permute-start(bf16[16,2048]{1,0:T(8,128)(2,1)S(1)} %get-tuple-element.315), channel_id=1, source_target_pairs={{0,1},{1,2},{2,3},{4,5},{5,6},{6,7},{8,9},{9,10},{10,11},{12,13},{... | collective-permute-start | bytes 196616 | tf_op jit(solution)/shard_map/while/body/eval_jaxpr/ppermute | solution.py:12
  126.2 6.2 %collective-permute-start = (bf16[16,2048]{1,0:T(8,128)(2,1)S(1)}, bf16[16,2048]{1,0:T(8,128)(2,1)S(1)}, u32[]{:S(2)}, u32[]{:S(2)}) collective-permute-start(bf16[16,2048]{1,0:T(8,128)(2,1)S(1)} %get-tuple-element.315), channel_id=1, source_target_pairs={{0,1},{1,2},{2,3},{4,5},{5,6},{6,7},{8,9},{9,10},{10,11},{12,13},{... | collective-permute-start | bytes 196616 | tf_op jit(solution)/shard_map/while/body/eval_jaxpr/ppermute | solution.py:12
Sparse Core Ops, SparseCore 0:
  9.2 59.2 all-gather.3
  133.3 42.8 all-reduce.1
where the time goes:
time: 185 us
  waiting for transfers between devices  94.3 us (51%)
  starting transfers between devices  36 us (19%)
  matrix products  19.8 us (11%)
  blocking collectives  14.7 us (8%)
  between operations  13.4 us (7%)
  other arithmetic  3.96 us (2%)
    psum x1, waiting for transfers between devices, broadcast(): return lax.psum(jnp.where(mine, x, jnp.zeros_like(x)), axis)  43 us
    ppermute x7, starting transfers between devices, from_behind(): return lax.ppermute(x, axis, pairs)  30.8 us
    all_gather x1, waiting for transfers between devices, body(): weight = lax.all_gather(tower_w[0], 'ingest', axis=0, tiled=True)  25.3 us
    dot_general x4, matrix products, tower_layer(): y = jnp.dot(normed, weight, preferred_element_type=jnp.float32)  18.6 us
    all_gather x1, blocking collectives, body(): blocks = lax.all_gather(pooled[None], 'section', axis=0, tiled=True)  14.7 us
    ppermute x7, waiting for transfers between devices, from_behind(): return lax.ppermute(x, axis, pairs)  12.8 us
    all_to_all x1, waiting for transfers between devices, body(): lax.all_to_all(buffer, 'ingest', split_axis=0, concat_axis=0, tiled=True)  12.4 us
    all_to_all x1, starting transfers between devices, body(): lax.all_to_all(buffer, 'ingest', split_axis=0, concat_axis=0, tiled=True)  5.16 us
  transfers between devices with their start and end apart: 10, of which 10 were waited for; matrix products, arithmetic and copies ran while one was open for 2% of the time, Pallas kernels for 0%

commit v1 on v0

--- a/solution.py
+++ b/solution.py
@@ -1,10 +1,15 @@
+import functools
+
 import jax
 import jax.numpy as jnp
 from jax import lax
+from jax.experimental import pallas as pl
+from jax.experimental.pallas import tpu as pltpu
 from jax.sharding import PartitionSpec as P
 
+MESH = pl.DeviceIdType.MESH
 CARD_DEV = 16
-
+LANES = 128
 
 def from_behind(x, axis, by):
     count = lax.axis_size(axis)
@@ -25,7 +30,7 @@
     return (u + jax.nn.silu(y)).astype(jnp.bfloat16)
 
 
-def body(txn_feats, txn_seg, seg_row, send_counts, gains, tower_w):
+def plain_body(txn_feats, txn_seg, seg_row, send_counts, gains, tower_w):
     width = txn_feats.shape[1]
     owners = lax.axis_size("ingest")
     sections = lax.axis_size("section")
@@ -77,6 +82,264 @@
     return lax.dynamic_index_in_dim(everything, section_pos, 0, keepdims=False)
 
 
+def tower_kernel(
+    owners, sections, cards,
+    seg_ref, row_ref, count_ref, gain_ref, feats_hbm, w_hbm, out_ref,
+    feats, w_all, parts, parts_in, pooled, xs, done, home,
+    local_sem, w_send, w_recv, p_send, p_recv, x_send, z_send, z_recv, a_send, a_recv, r_send, r_recv,
+):
+    me = lax.axis_index("ingest")
+    sec = lax.axis_index("section")
+    devices = owners * sections
+    flat = me * sections + sec
+    width = feats.shape[1]
+    fb = width // owners
+    rows = owners * cards
+    slots = row_ref.shape[1]
+    core = lax.rem(me, 2)
+    sibling = me + 1 - 2 * core
+    chip = me // 2
+    chips = owners // 2
+
+    def remote(src, dst, send, recv, to):
+        return pltpu.make_async_remote_copy(
+            src_ref=src, dst_ref=dst, send_sem=send, recv_sem=recv, device_id=to, device_id_type=MESH
+        )
+
+    def cols(k):
+        return pl.ds(pl.multiple_of(k * fb, LANES), fb)
+
+    feats_copy = pltpu.make_async_copy(feats_hbm, feats, local_sem.at[0])
+    feats_copy.start()
+    w_copy = pltpu.make_async_copy(w_hbm.at[0, :, cols(me)], w_all.at[me], local_sem.at[1])
+    w_copy.start()
+
+    barrier = pltpu.get_barrier_semaphore()
+
+    def greet(t, carry):
+        other = lax.rem(flat + t, devices)
+        pl.semaphore_signal(
+            barrier, inc=1, device_id=(other // sections, lax.rem(other, sections)), device_id_type=MESH
+        )
+        return carry
+
+    lax.fori_loop(1, devices, greet, 0)
+
+    seg = seg_ref[...]
+    owner = jnp.zeros_like(seg)
+    end = count_ref[0, 0]
+    for j in range(owners):
+        if j > 0:
+            end = end + count_ref[0, j]
+        owner = owner + (seg >= end).astype(jnp.int32)
+    row = jnp.zeros_like(seg)
+    for g in range(slots):
+        row = jnp.where(seg == g, row_ref[0, g], row)
+    target = owner * cards + row
+    ids = lax.broadcasted_iota(jnp.int32, (rows, seg.shape[1]), 0)
+    place = jnp.where(ids == target, 1.0, 0.0).astype(jnp.bfloat16)
+    feats_copy.wait()
+    for k in range(owners):
+        parts[k] = jnp.dot(
+            place, feats[:, k * fb : (k + 1) * fb], preferred_element_type=jnp.float32
+        ).astype(jnp.bfloat16)
+    pl.semaphore_wait(barrier, devices - 1)
+
+    def part_copy(t):
+        to = lax.rem(me + t, owners)
+        return remote(parts.at[to], parts_in.at[me], p_send.at[t], p_recv.at[me], (to, sec))
+
+    def weight_copy(t):
+        to = lax.rem(me + t, owners)
+        return remote(w_hbm.at[0, :, cols(to)], w_all.at[me], w_send.at[t], w_recv.at[me], (to, sec))
+
+    for t in range(1, owners):
+        part_copy(t).start()
+    for t in range(1, owners):
+        weight_copy(t).start()
+
+    total = parts[me].astype(jnp.float32)
+    for t in range(1, owners):
+        frm = lax.rem(me + owners - t, owners)
+        remote(parts.at[me], parts_in.at[frm], p_send.at[t], p_recv.at[frm], (frm, sec)).wait_recv()
+        total = total + parts_in[frm].astype(jnp.float32)
+    pooled[...] = total.astype(jnp.bfloat16)
+
+    def entry_copy():
+        return remote(pooled, xs.at[sec, me], x_send.at[0], z_recv.at[sec], (me, 0))
+
+    @pl.when(sec == 0)
+    def _():
+        xs[0, me] = pooled[...]
+
+    @pl.when(sec > 0)
+    def _():
+        entry_copy().start()
+
+    w_copy.wait()
+    for t in range(1, owners):
+        frm = lax.rem(me + owners - t, owners)
+        remote(w_all.at[me], w_all.at[frm], w_send.at[t], w_recv.at[frm], (frm, sec)).wait_recv()
+
+    def own_copy(m):
+        block = xs.at[m, me]
+        return remote(block, block, a_send.at[m, 0], a_recv.at[m, me], (sibling, sec))
+
+    def cross_copy(m, d):
+        block = xs.at[m, me]
+        to = lax.rem(chip + d, chips) * 2 + core
+        return remote(block, block, a_send.at[m, d], a_recv.at[m, me], (to, sec))
+
+    def pass_copy(m, d):
+        frm = lax.rem(chip + chips - d, chips) * 2 + core
+        block = xs.at[m, frm]
+        return remote(block, block, a_send.at[m, chips - 1 + d], a_recv.at[m, frm], (sibling, sec))
+
+    def arrive(m, k):
+        block = xs.at[m, k]
+        remote(block, block, a_send.at[m, 0], a_recv.at[m, k], (sibling, sec)).wait_recv()
+
+    def next_copy(m):
+        return remote(done.at[m], xs.at[m, me], z_send.at[m], z_recv.at[m], (me, sec + 1))
+
+    def home_copy(m, j):
+        piece = done.at[m, pl.ds(j * cards, cards)]
+        return remote(piece, home.at[me], r_send.at[m, j], r_recv.at[me], (j, m))
+
+    last = sections - 1
+
+    def each(m, carry):
+        @pl.when(sec + m > 0)
+        def _():
+            block = xs.at[m, me]
+            remote(block, block, z_send.at[m], z_recv.at[m], (me, 0)).wait_recv()
+
+        for d in range(1, chips):
+            cross_copy(m, d).start()
+        own_copy(m).start()
+
+        def term(k, acc, sq):
+            u = xs[m, k].astype(jnp.float32)
+            h = (u * gain_ref[:, cols(k)]).astype(jnp.bfloat16)
+            acc = acc + jnp.dot(h, w_all[k], preferred_element_type=jnp.float32)
+            return acc, sq + jnp.sum(u * u, axis=1, keepdims=True)
+
+        acc = jnp.zeros((rows, fb), jnp.float32)
+        sq = jnp.zeros((rows, 1), jnp.float32)
+        acc, sq = term(me, acc, sq)
+        arrive(m, sibling)
+        acc, sq = term(sibling, acc, sq)
+        for d in range(1, chips):
+            k = lax.rem(chip + chips - d, chips) * 2 + core
+            arrive(m, k)
+            pass_copy(m, d).start()
+            acc, sq = term(k, acc, sq)
+        for d in range(1, chips):
+            k = lax.rem(chip + chips - d, chips) * 2 + 1 - core
+            arrive(m, k)
+            acc, sq = term(k, acc, sq)
+        y = acc * lax.rsqrt(sq / width + 1e-05)
+        u = xs[m, me].astype(jnp.float32)
+        done[m] = (u + y / (1.0 + jnp.exp(-y))).astype(jnp.bfloat16)
+
+        @pl.when(sec < last)
+        def _():
+            next_copy(m).start()
+
+        @pl.when(sec == last)
+        def _():
+            for j in range(owners):
+                @pl.when((m < last) | (me != j))
+                def _():
+                    home_copy(m, j).start()
+
+        return carry
+
+    lax.fori_loop(0, sections, each, 0)
+
+    for k in range(owners):
+        @pl.when((sec != last) | (me != k))
+        def _():
+            remote(home.at[k], home.at[k], r_send.at[0, 0], r_recv.at[k], (k, last)).wait_recv()
+            out_ref[:, k * fb : (k + 1) * fb] = home[k]
+
+        @pl.when((sec == last) & (me == k))
+        def _():
+            out_ref[:, k * fb : (k + 1) * fb] = done[sections - 1, k * cards : (k + 1) * cards]
+
+    for t in range(1, owners):
+        part_copy(t).wait_send()
+        weight_copy(t).wait_send()
+
+    @pl.when(sec > 0)
+    def _():
+        entry_copy().wait_send()
+
+    def finish(m, carry):
+        own_copy(m).wait_send()
+        for d in range(1, chips):
+            cross_copy(m, d).wait_send()
+            pass_copy(m, d).wait_send()
+
+        @pl.when(sec < last)
+        def _():
+            next_copy(m).wait_send()
+
+        @pl.when(sec == last)
+        def _():
+            for j in range(owners):
+                @pl.when((m < last) | (me != j))
+                def _():
+                    home_copy(m, j).wait_send()
+
+        return carry
+
+    lax.fori_loop(0, sections, finish, 0)
+
+
+def kernel_body(owners, sections, txn_feats, txn_seg, seg_row, send_counts, gains, tower_w):
+    width = txn_feats.shape[1]
+    fb = width // owners
+    cards = CARD_DEV
+    rows = owners * cards
+    bf = jnp.bfloat16
+    vmem = pl.BlockSpec(memory_space=pltpu.VMEM)
+    smem = pl.BlockSpec(memory_space=pltpu.SMEM)
+    anywhere = pl.BlockSpec(memory_space=pl.ANY)
+    dma = pltpu.SemaphoreType.DMA
+    return pl.pallas_call(
+        functools.partial(tower_kernel, owners, sections, cards),
+        out_shape=jax.ShapeDtypeStruct((cards, width), bf),
+        in_specs=[vmem, smem, smem, vmem, anywhere, anywhere],
+        out_specs=vmem,
+        scratch_shapes=[
+            pltpu.VMEM(txn_feats.shape, bf),
+            pltpu.VMEM((owners, fb, fb), bf),
+            pltpu.VMEM((owners, rows, fb), bf),
+            pltpu.VMEM((owners, rows, fb), bf),
+            pltpu.VMEM((rows, fb), bf),
+            pltpu.VMEM((sections, owners, rows, fb), bf),
+            pltpu.VMEM((sections, rows, fb), bf),
+            pltpu.VMEM((owners, cards, fb), bf),
+            dma((2,)),
+            dma((owners,)),
+            dma((owners,)),
+            dma((owners,)),
+            dma((owners,)),
+            dma((1,)),
+            dma((sections,)),
+            dma((sections,)),
+            dma((sections, owners)),
+            dma((sections, owners)),
+            dma((sections, owners)),
+            dma((owners,)),
+        ],
+        compiler_params=pltpu.CompilerParams(
+            collective_id=0, has_side_effects=True, vmem_limit_bytes=32 * 1024 * 1024
+        ),
+    )(txn_seg, seg_row, send_counts, gains, txn_feats, tower_w)
+
+
 def solution(mesh):
     in_specs = (
         P(("ingest", "section"), None),
@@ -87,4 +350,12 @@
         P("section", "ingest", None),
     )
     out_specs = P(("ingest", "section"), None)
+    owners, sections = mesh.shape["ingest"], mesh.shape["section"]
+
+    def body(txn_feats, txn_seg, seg_row, send_counts, gains, tower_w):
+        args = (txn_feats, txn_seg, seg_row, send_counts, gains, tower_w)
+        if owners % 2 == 0 and txn_feats.shape[1] % (owners * LANES) == 0:
+            return kernel_body(owners, sections, *args)
+        return plain_body(*args)
+
     return jax.shard_map(body, mesh=mesh, in_specs=in_specs, out_specs=out_specs, check_vma=False)

time: 185 us -> 85.5 us (0.46)
  the two profiles are of different devices: /device:TPU:0 before, /device:TPU:25 now
where the time goes in v1:
time: 85.5 us; the launch traced here: 85.2 us
  Pallas kernels  79.4 us (93%)
  local copies, waits for them, and re-layouts  5.76 us (7%)
    pallas_call x1, Pallas kernels, kernel_body(): pl.pallas_call(functools.partial(tower_kernel, owners, sections, cards),...  79.4 us
    unnamed x13, local copies, waits for them, and re-layouts  5.76 us

profile of v1, /device:TPU:25, one launch (start us, length us, event | category | flops | bytes accessed | tf_op | source)
XLA Modules:
  0.0 85.2 jit_solution(368872254199663650)
XLA Ops:
  0.0 0.0 copy-start
  0.0 1.2 %copy-done = bf16[256,2048]{1,0:T(8,128)(2,1)S(1)} copy-done((bf16[256,2048]{1,0:T(8,128)(2,1)S(1)}, bf16[256,2048]{1,0:T(8,128)(2,1)}, u32[]{:S(2)}) %copy-start) | copy-done | bytes 1048600
  1.2 0.0 copy-start.1
  1.2 1.2 %copy-done.1 = bf16[1,256,2048]{2,1,0:T(8,128)(2,1)S(1)} copy-done((bf16[1,256,2048]{2,1,0:T(8,128)(2,1)S(1)}, bf16[1,256,2048]{2,1,0:T(8,128)(2,1)}, u32[]{:S(2)}) %copy-start.1) | copy-done | bytes 1048600
  2.5 0.0 copy-start.2
  2.5 0.7 copy-done.2
  3.1 0.0 copy-start.3
  3.2 0.7 copy-done.3
  3.8 0.0 copy-start.4
  3.8 0.7 copy-done.4
  4.5 0.0 copy-start.5
  4.5 0.7 copy-done.5
  5.1 79.4 %shard_map.64 = bf16[16,2048]{1,0:T(8,128)(2,1)S(1)} custom-call(s32[1,256]{1,0:T(1,128)S(1)} %copy-done.3, s32[1,64]{1,0:T(1,128)S(1)} %copy-done.4, s32[1,8]{1,0:T(1,128)S(1)} %copy-done.5, f32[1,2048]{1,0:T(1,128)S(1)} %copy-done.2, bf16[256,2048]{1,0:T(8,128)(2,1)S(1)} %copy-done, bf16[1,256,2048]{2,1,0:T(8,128)(2,1)S(1)} %copy-done.1), custom_call_target="tpu_custom_call" | custom-call | tf_op jit(solution)/shard_map/pallas_call | solution.py:310
  84.6 0.6 copy.8
Async XLA Ops:
  0.0 1.2 %copy-start = (bf16[256,2048]{1,0:T(8,128)(2,1)S(1)}, bf16[256,2048]{1,0:T(8,128)(2,1)}, u32[]{:S(2)}) copy-start(bf16[256,2048]{1,0:T(8,128)(2,1)} %feats_hbm.1) | copy-start | bytes 3145732
  1.2 1.2 %copy-start.1 = (bf16[1,256,2048]{2,1,0:T(8,128)(2,1)S(1)}, bf16[1,256,2048]{2,1,0:T(8,128)(2,1)}, u32[]{:S(2)}) copy-start(bf16[1,256,2048]{2,1,0:T(8,128)(2,1)} %w_hbm.1) | copy-start | bytes 3145732
  2.5 0.7 copy-start.2
  3.1 0.7 copy-start.3
  3.8 0.7 copy-start.4
  4.5 0.7 copy-start.5

commit v2 on v1

--- a/solution.py
+++ b/solution.py
@@ -84,12 +84,15 @@
 
 def tower_kernel(
     owners, sections, cards,
-    seg_ref, row_ref, count_ref, gain_ref, feats_hbm, w_hbm, out_ref,
-    feats, w_all, parts, parts_in, pooled, xs, done, home,
-    local_sem, w_send, w_recv, p_send, p_recv, x_send, z_send, z_recv, a_send, a_recv, r_send, r_recv,
+    seg_hbm, row_hbm, count_hbm, gain_hbm, feats_hbm, w_hbm, out_ref,
+    seg_ref, row_ref, count_ref, gain_ref, feats, weight,
+    sib_out, sib_in, own, cross_out, cross_in, sq_out, sq_in, pooled, xs, done, home,
+    local_sem, sib_send, sib_recv, cross_send, cross_recv, sq_send, sq_recv,
+    x_send, z_send, z_recv, r_send, r_recv,
 ):
     me = lax.axis_index("ingest")
     sec = lax.axis_index("section")
+    last = sections - 1
     devices = owners * sections
     flat = me * sections + sec
     width = feats.shape[1]
@@ -109,10 +112,15 @@
     def cols(k):
         return pl.ds(pl.multiple_of(k * fb, LANES), fb)
 
-    feats_copy = pltpu.make_async_copy(feats_hbm, feats, local_sem.at[0])
-    feats_copy.start()
-    w_copy = pltpu.make_async_copy(w_hbm.at[0, :, cols(me)], w_all.at[me], local_sem.at[1])
-    w_copy.start()
+    loads = [
+        pltpu.make_async_copy(source, to, local_sem.at[n])
+        for n, (source, to) in enumerate((
+            (seg_hbm, seg_ref), (row_hbm, row_ref), (count_hbm, count_ref),
+            (feats_hbm, feats), (gain_hbm.at[:, cols(me)], gain_ref), (w_hbm.at[0], weight),
+        ))
+    ]
+    for load in loads:
+        load.start()
 
     barrier = pltpu.get_barrier_semaphore()
 
@@ -124,6 +132,8 @@
         return carry
 
     lax.fori_loop(1, devices, greet, 0)
+    for load in loads[:3]:
+        load.wait()
 
     seg = seg_ref[...]
     owner = jnp.zeros_like(seg)
@@ -138,108 +148,111 @@
     target = owner * cards + row
     ids = lax.broadcasted_iota(jnp.int32, (rows, seg.shape[1]), 0)
     place = jnp.where(ids == target, 1.0, 0.0).astype(jnp.bfloat16)
-    feats_copy.wait()
-    for k in range(owners):
-        parts[k] = jnp.dot(
-            place, feats[:, k * fb : (k + 1) * fb], preferred_element_type=jnp.float32
-        ).astype(jnp.bfloat16)
+    loads[3].wait()
     pl.semaphore_wait(barrier, devices - 1)
 
-    def part_copy(t):
-        to = lax.rem(me + t, owners)
-        return remote(parts.at[to], parts_in.at[me], p_send.at[t], p_recv.at[me], (to, sec))
-
-    def weight_copy(t):
-        to = lax.rem(me + t, owners)
-        return remote(w_hbm.at[0, :, cols(to)], w_all.at[me], w_send.at[t], w_recv.at[me], (to, sec))
-
-    for t in range(1, owners):
-        part_copy(t).start()
-    for t in range(1, owners):
-        weight_copy(t).start()
-
-    total = parts[me].astype(jnp.float32)
-    for t in range(1, owners):
-        frm = lax.rem(me + owners - t, owners)
-        remote(parts.at[me], parts_in.at[frm], p_send.at[t], p_recv.at[frm], (frm, sec)).wait_recv()
-        total = total + parts_in[frm].astype(jnp.float32)
-    pooled[...] = total.astype(jnp.bfloat16)
+    def ahead(d):
+        return lax.rem(chip + d, chips)
+
+    def behind(d):
+        return lax.rem(chip + chips - d, chips)
+
+    def sib_copy(q, d):
+        c = ahead(d)
+        return remote(sib_out.at[q, c], sib_in.at[q, c], sib_send.at[q, d], sib_recv.at[q, c], (sibling, sec))
+
+    def cross_copy(q, d):
+        return remote(
+            cross_out.at[q, d], cross_in.at[q, chip], cross_send.at[q, d], cross_recv.at[q, chip],
+            (ahead(d) * 2 + core, sec),
+        )
+
+    def cross_wait(q, d):
+        c = behind(d)
+        remote(
+            cross_out.at[q, d], cross_in.at[q, c], cross_send.at[q, d], cross_recv.at[q, c], (c * 2 + core, sec)
+        ).wait_recv()
+
+    order = list(range(1, chips)) + [0]
+
+    def reduced(q, product):
+        for d in order:
+            c = ahead(d)
+            sib_out[q, c] = product(c * 2 + 1 - core).astype(jnp.bfloat16)
+            sib_copy(q, d).start()
+        for d in order:
+            c = ahead(d)
+            own[d] = product(c * 2 + core)
+        for d in order[:-1]:
+            sib_copy(q, d).wait_recv()
+            cross_out[q, d] = (own[d] + sib_in[q, ahead(d)].astype(jnp.float32)).astype(jnp.bfloat16)
+            cross_copy(q, d).start()
+        sib_copy(q, 0).wait_recv()
+        total = own[0] + sib_in[q, chip].astype(jnp.float32)
+        for d in order[:-1]:
+            cross_wait(q, d)
+            total = total + cross_in[q, behind(d)].astype(jnp.float32)
+        return total
+
+    def reduced_sends(q):
+        for d in order:
+            sib_copy(q, d).wait_send()
+        for d in order[:-1]:
+            cross_copy(q, d).wait_send()
+
+    x0 = reduced(
+        sections, lambda k: jnp.dot(place, feats[:, cols(k)], preferred_element_type=jnp.float32)
+    ).astype(jnp.bfloat16)
 
     def entry_copy():
-        return remote(pooled, xs.at[sec, me], x_send.at[0], z_recv.at[sec], (me, 0))
+        return remote(pooled, xs.at[sec], x_send.at[0], z_recv.at[sec], (me, 0))
 
     @pl.when(sec == 0)
     def _():
-        xs[0, me] = pooled[...]
+        xs[0] = x0
 
     @pl.when(sec > 0)
     def _():
+        pooled[...] = x0
         entry_copy().start()
 
-    w_copy.wait()
-    for t in range(1, owners):
+    loads[4].wait()
+    loads[5].wait()
+
+    def sq_copy(m, t):
+        to = lax.rem(me + t, owners)
+        return remote(sq_out.at[m], sq_in.at[m, me], sq_send.at[m, t], sq_recv.at[m, me], (to, sec))
+
+    def sq_wait(m, t):
         frm = lax.rem(me + owners - t, owners)
-        remote(w_all.at[me], w_all.at[frm], w_send.at[t], w_recv.at[frm], (frm, sec)).wait_recv()
-
-    def own_copy(m):
-        block = xs.at[m, me]
-        return remote(block, block, a_send.at[m, 0], a_recv.at[m, me], (sibling, sec))
-
-    def cross_copy(m, d):
-        block = xs.at[m, me]
-        to = lax.rem(chip + d, chips) * 2 + core
-        return remote(block, block, a_send.at[m, d], a_recv.at[m, me], (to, sec))
-
-    def pass_copy(m, d):
-        frm = lax.rem(chip + chips - d, chips) * 2 + core
-        block = xs.at[m, frm]
-        return remote(block, block, a_send.at[m, chips - 1 + d], a_recv.at[m, frm], (sibling, sec))
-
-    def arrive(m, k):
-        block = xs.at[m, k]
-        remote(block, block, a_send.at[m, 0], a_recv.at[m, k], (sibling, sec)).wait_recv()
+        remote(sq_out.at[m], sq_in.at[m, frm], sq_send.at[m, t], sq_recv.at[m, frm], (frm, sec)).wait_recv()
+        return sq_in[m, frm]
 
     def next_copy(m):
-        return remote(done.at[m], xs.at[m, me], z_send.at[m], z_recv.at[m], (me, sec + 1))
+        return remote(done.at[m], xs.at[m], z_send.at[m], z_recv.at[m], (me, sec + 1))
 
     def home_copy(m, j):
         piece = done.at[m, pl.ds(j * cards, cards)]
         return remote(piece, home.at[me], r_send.at[m, j], r_recv.at[me], (j, m))
 
-    last = sections - 1
-
     def each(m, carry):
         @pl.when(sec + m > 0)
         def _():
-            block = xs.at[m, me]
-            remote(block, block, z_send.at[m], z_recv.at[m], (me, 0)).wait_recv()
-
-        for d in range(1, chips):
-            cross_copy(m, d).start()
-        own_copy(m).start()
-
-        def term(k, acc, sq):
-            u = xs[m, k].astype(jnp.float32)
-            h = (u * gain_ref[:, cols(k)]).astype(jnp.bfloat16)
-            acc = acc + jnp.dot(h, w_all[k], preferred_element_type=jnp.float32)
-            return acc, sq + jnp.sum(u * u, axis=1, keepdims=True)
-
-        acc = jnp.zeros((rows, fb), jnp.float32)
-        sq = jnp.zeros((rows, 1), jnp.float32)
-        acc, sq = term(me, acc, sq)
-        arrive(m, sibling)
-        acc, sq = term(sibling, acc, sq)
-        for d in range(1, chips):
-            k = lax.rem(chip + chips - d, chips) * 2 + core
-            arrive(m, k)
-            pass_copy(m, d).start()
-            acc, sq = term(k, acc, sq)
-        for d in range(1, chips):
-            k = lax.rem(chip + chips - d, chips) * 2 + 1 - core
-            arrive(m, k)
-            acc, sq = term(k, acc, sq)
-        y = acc * lax.rsqrt(sq / width + 1e-05)
-        u = xs[m, me].astype(jnp.float32)
+            remote(xs.at[m], xs.at[m], z_send.at[m], z_recv.at[m], (me, 0)).wait_recv()
+
+        u = xs[m].astype(jnp.float32)
+        h = (u * gain_ref[...]).astype(jnp.bfloat16)
+        sq = jnp.broadcast_to(jnp.sum(u * u, axis=1, keepdims=True), (rows, LANES))
+        sq_out[m] = jnp.transpose(sq)[:8]
+        for t in range(1, owners):
+            sq_copy(m, t).start()
+        y = reduced(m, lambda k: jnp.dot(h, weight[:, cols(k)], preferred_element_type=jnp.float32))
+        sq = sq_out[m]
+        for t in range(1, owners):
+            sq = sq + sq_wait(m, t)
+        scale = lax.rsqrt(sq / width + 1e-05)
+        y = y * jnp.transpose(scale)[:, :1]
+        u = xs[m].astype(jnp.float32)
         done[m] = (u + y / (1.0 + jnp.exp(-y))).astype(jnp.bfloat16)
 
         @pl.when(sec < last)
@@ -265,21 +278,18 @@
 
         @pl.when((sec == last) & (me == k))
         def _():
-            out_ref[:, k * fb : (k + 1) * fb] = done[sections - 1, k * cards : (k + 1) * cards]
-
-    for t in range(1, owners):
-        part_copy(t).wait_send()
-        weight_copy(t).wait_send()
+            out_ref[:, k * fb : (k + 1) * fb] = done[last, k * cards : (k + 1) * cards]
+
+    reduced_sends(sections)
 
     @pl.when(sec > 0)
     def _():
         entry_copy().wait_send()
 
     def finish(m, carry):
-        own_copy(m).wait_send()
-        for d in range(1, chips):
-            cross_copy(m, d).wait_send()
-            pass_copy(m, d).wait_send()
+        reduced_sends(m)
+        for t in range(1, owners):
+            sq_copy(m, t).wait_send()
 
         @pl.when(sec < last)
         def _():
@@ -302,40 +312,49 @@
     fb = width // owners
     cards = CARD_DEV
     rows = owners * cards
+    chips = owners // 2
     bf = jnp.bfloat16
-    vmem = pl.BlockSpec(memory_space=pltpu.VMEM)
-    smem = pl.BlockSpec(memory_space=pltpu.SMEM)
-    anywhere = pl.BlockSpec(memory_space=pl.ANY)
+    hbm = pl.BlockSpec(memory_space=pltpu.HBM)
     dma = pltpu.SemaphoreType.DMA
+    stages = sections + 1
     return pl.pallas_call(
         functools.partial(tower_kernel, owners, sections, cards),
         out_shape=jax.ShapeDtypeStruct((cards, width), bf),
-        in_specs=[vmem, smem, smem, vmem, anywhere, anywhere],
-        out_specs=vmem,
+        in_specs=[hbm] * 6,
+        out_specs=pl.BlockSpec(memory_space=pltpu.VMEM),
         scratch_shapes=[
+            pltpu.VMEM(txn_seg.shape, jnp.int32),
+            pltpu.SMEM(seg_row.shape, jnp.int32),
+            pltpu.SMEM(send_counts.shape, jnp.int32),
+            pltpu.VMEM((1, fb), jnp.float32),
             pltpu.VMEM(txn_feats.shape, bf),
-            pltpu.VMEM((owners, fb, fb), bf),
-            pltpu.VMEM((owners, rows, fb), bf),
-            pltpu.VMEM((owners, rows, fb), bf),
+            pltpu.VMEM((fb, width), bf),
+            pltpu.VMEM((stages, chips, rows, fb), bf),
+            pltpu.VMEM((stages, chips, rows, fb), bf),
+            pltpu.VMEM((chips, rows, fb), jnp.float32),
+            pltpu.VMEM((stages, chips, rows, fb), bf),
+            pltpu.VMEM((stages, chips, rows, fb), bf),
+            pltpu.VMEM((sections, 8, rows), jnp.float32),
+            pltpu.VMEM((sections, owners, 8, rows), jnp.float32),
             pltpu.VMEM((rows, fb), bf),
-            pltpu.VMEM((sections, owners, rows, fb), bf),
+            pltpu.VMEM((sections, rows, fb), bf),
             pltpu.VMEM((sections, rows, fb), bf),
             pltpu.VMEM((owners, cards, fb), bf),
-            dma((2,)),
-            dma((owners,)),
-            dma((owners,)),
-            dma((owners,)),
-            dma((owners,)),
+            dma((6,)),
+            dma((stages, chips)),
+            dma((stages, chips)),
+            dma((stages, chips)),
+            dma((stages, chips)),
+            dma((sections, owners)),
+            dma((sections, owners)),
             dma((1,)),
             dma((sections,)),
             dma((sections,)),
             dma((sections, owners)),
-            dma((sections, owners)),
-            dma((sections, owners)),
             dma((owners,)),
         ],
         compiler_params=pltpu.CompilerParams(
-            collective_id=0, has_side_effects=True, vmem_limit_bytes=32 * 1024 * 1024
+            collective_id=0, has_side_effects=True, vmem_limit_bytes=64 * 1024 * 1024
         ),
     )(txn_seg, seg_row, send_counts, gains, txn_feats, tower_w)
 
@@ -354,7 +373,7 @@
 
     def body(txn_feats, txn_seg, seg_row, send_counts, gains, tower_w):
         args = (txn_feats, txn_seg, seg_row, send_counts, gains, tower_w)
-        if owners % 2 == 0 and txn_feats.shape[1] % (owners * LANES) == 0:
+        if owners % 2 == 0 and owners * CARD_DEV % LANES == 0 and txn_feats.shape[1] % (owners * LANES) == 0:
             return kernel_body(owners, sections, *args)
         return plain_body(*args)
 

time: 85.5 us -> 75.3 us (0.88)
  Pallas kernels: 79.4 us -> 73.6 us
  local copies, waits for them, and re-layouts: 5.76 us -> 1.47 us
    pallas_call x1, Pallas kernels: 79.4 us -> 73.6 us  [kernel_body(): pl.pallas_call(functools.partial(tower_kernel, owners, sections, cards),...]
    unnamed x13 -> x1, local copies, waits for them, and re-layouts: 5.76 us -> 1.47 us
where the time goes in v2:
time: 75.3 us; the launch traced here: 75.1 us
  Pallas kernels  73.6 us (98%)
  local copies, waits for them, and re-layouts  1.47 us (2%)
    pallas_call x1, Pallas kernels, kernel_body(): pl.pallas_call(functools.partial(tower_kernel, owners, sections, cards),...  73.6 us

profile of v2, /device:TPU:25, one launch (start us, length us, event | category | flops | bytes accessed | tf_op | source)
XLA Modules:
  0.0 75.1 jit_solution(15030528821100404151)
XLA Ops:
  0.0 73.6 %shard_map.64 = bf16[16,2048]{1,0:T(8,128)(2,1)} custom-call(s32[1,256]{1,0:T(1,128)} %seg_hbm.1, s32[1,64]{1,0:T(1,128)} %row_hbm.1, s32[1,8]{1,0:T(1,128)} %count_hbm.1, f32[1,2048]{1,0:T(1,128)} %gain_hbm.1, bf16[256,2048]{1,0:T(8,128)(2,1)} %feats_hbm.1, bf16[1,256,2048]{2,1,0:T(8,128)(2,1)} %w_hbm.1), custom_call_target="tpu_custom_call" | custom-call | tf_op jit(solution)/shard_map/pallas_call | solution.py:320
  73.6 1.5 %copy.8 = bf16[16,2048]{1,0:T(8,128)(2,1)} copy(bf16[16,2048]{1,0:T(8,128)(2,1)} %shard_map.64) | data formatting | bytes 131072

commit v3 on v2

--- a/solution.py
+++ b/solution.py
@@ -86,15 +86,13 @@
     owners, sections, cards,
     seg_hbm, row_hbm, count_hbm, gain_hbm, feats_hbm, w_hbm, out_ref,
     seg_ref, row_ref, count_ref, gain_ref, feats, weight,
-    sib_out, sib_in, own, cross_out, cross_in, sq_out, sq_in, pooled, xs, done, home,
+    sib_out, sib_in, own, cross_out, cross_in, sq_out, sq_in, pooled, xs, done, back, home,
     local_sem, sib_send, sib_recv, cross_send, cross_recv, sq_send, sq_recv,
-    x_send, z_send, z_recv, r_send, r_recv,
+    x_send, z_send, z_recv, b_send, b_recv, r_send, r_recv,
 ):
     me = lax.axis_index("ingest")
     sec = lax.axis_index("section")
     last = sections - 1
-    devices = owners * sections
-    flat = me * sections + sec
     width = feats.shape[1]
     fb = width // owners
     rows = owners * cards
@@ -124,14 +122,14 @@
 
     barrier = pltpu.get_barrier_semaphore()
 
-    def greet(t, carry):
-        other = lax.rem(flat + t, devices)
+    for t in range(1, owners):
         pl.semaphore_signal(
-            barrier, inc=1, device_id=(other // sections, lax.rem(other, sections)), device_id_type=MESH
-        )
-        return carry
-
-    lax.fori_loop(1, devices, greet, 0)
+            barrier, inc=1, device_id=(lax.rem(me + t, owners), sec), device_id_type=MESH
+        )
+    for t in range(1, sections):
+        pl.semaphore_signal(
+            barrier, inc=1, device_id=(me, lax.rem(sec + t, sections)), device_id_type=MESH
+        )
     for load in loads[:3]:
         load.wait()
 
@@ -149,7 +147,7 @@
     ids = lax.broadcasted_iota(jnp.int32, (rows, seg.shape[1]), 0)
     place = jnp.where(ids == target, 1.0, 0.0).astype(jnp.bfloat16)
     loads[3].wait()
-    pl.semaphore_wait(barrier, devices - 1)
+    pl.semaphore_wait(barrier, owners + sections - 2)
 
     def ahead(d):
         return lax.rem(chip + d, chips)
@@ -231,9 +229,13 @@
     def next_copy(m):
         return remote(done.at[m], xs.at[m], z_send.at[m], z_recv.at[m], (me, sec + 1))
 
-    def home_copy(m, j):
-        piece = done.at[m, pl.ds(j * cards, cards)]
-        return remote(piece, home.at[me], r_send.at[m, j], r_recv.at[me], (j, m))
+    def back_copy(m):
+        return remote(done.at[m], back, b_send.at[m], b_recv.at[0], (me, m))
+
+    def home_copy(t):
+        to = lax.rem(me + t, owners)
+        piece = back.at[pl.ds(to * cards, cards)]
+        return remote(piece, home.at[me], r_send.at[t], r_recv.at[me], (to, sec))
 
     def each(m, carry):
         @pl.when(sec + m > 0)
@@ -259,26 +261,30 @@
         def _():
             next_copy(m).start()
 
-        @pl.when(sec == last)
-        def _():
-            for j in range(owners):
-                @pl.when((m < last) | (me != j))
-                def _():
-                    home_copy(m, j).start()
+        @pl.when((sec == last) & (m < last))
+        def _():
+            back_copy(m).start()
 
         return carry
 
     lax.fori_loop(0, sections, each, 0)
 
-    for k in range(owners):
-        @pl.when((sec != last) | (me != k))
-        def _():
-            remote(home.at[k], home.at[k], r_send.at[0, 0], r_recv.at[k], (k, last)).wait_recv()
-            out_ref[:, k * fb : (k + 1) * fb] = home[k]
-
-        @pl.when((sec == last) & (me == k))
-        def _():
-            out_ref[:, k * fb : (k + 1) * fb] = done[last, k * cards : (k + 1) * cards]
+    @pl.when(sec == last)
+    def _():
+        back[...] = done[last]
+
+    @pl.when(sec < last)
+    def _():
+        remote(back, back, b_send.at[0], b_recv.at[0], (me, last)).wait_recv()
+
+    for t in range(1, owners):
+        home_copy(t).start()
+    out_ref[:, cols(me)] = back[pl.ds(me * cards, cards)]
+    for t in range(1, owners):
+        frm = lax.rem(me + owners - t, owners)
+        remote(home.at[frm], home.at[frm], r_send.at[t], r_recv.at[frm], (frm, sec)).wait_recv()
+        out_ref[:, cols(frm)] = home[frm]
+        home_copy(t).wait_send()
 
     reduced_sends(sections)
 
@@ -295,12 +301,9 @@
         def _():
             next_copy(m).wait_send()
 
-        @pl.when(sec == last)
-        def _():
-            for j in range(owners):
-                @pl.when((m < last) | (me != j))
-                def _():
-                    home_copy(m, j).wait_send()
+        @pl.when((sec == last) & (m < last))
+        def _():
+            back_copy(m).wait_send()
 
         return carry
 
@@ -339,6 +342,7 @@
             pltpu.VMEM((rows, fb), bf),
             pltpu.VMEM((sections, rows, fb), bf),
             pltpu.VMEM((sections, rows, fb), bf),
+            pltpu.VMEM((rows, fb), bf),
             pltpu.VMEM((owners, cards, fb), bf),
             dma((6,)),
             dma((stages, chips)),
@@ -350,7 +354,9 @@
             dma((1,)),
             dma((sections,)),
             dma((sections,)),
-            dma((sections, owners)),
+            dma((sections,)),
+            dma((1,)),
+            dma((owners,)),
             dma((owners,)),
         ],
         compiler_params=pltpu.CompilerParams(

time: 75.3 us -> 73.8 us (0.980)
  Pallas kernels: 73.6 us -> 72.2 us
    pallas_call x1, Pallas kernels: 73.6 us -> 72.2 us  [kernel_body(): pl.pallas_call(functools.partial(tower_kernel, owners, sections, cards),...]
where the time goes in v3:
time: 73.8 us; the launch traced here: 73.6 us
  Pallas kernels  72.2 us (98%)
  local copies, waits for them, and re-layouts  1.47 us (2%)
    pallas_call x1, Pallas kernels, kernel_body(): pl.pallas_call(functools.partial(tower_kernel, owners, sections, cards),...  72.2 us

profile of v3, /device:TPU:25, one launch (start us, length us, event | category | flops | bytes accessed | tf_op | source)
XLA Modules:
  0.0 73.6 jit_solution(10568460599395863628)
XLA Ops:
  0.0 72.2 %shard_map.64 = bf16[16,2048]{1,0:T(8,128)(2,1)} custom-call(s32[1,256]{1,0:T(1,128)} %seg_hbm.1, s32[1,64]{1,0:T(1,128)} %row_hbm.1, s32[1,8]{1,0:T(1,128)} %count_hbm.1, f32[1,2048]{1,0:T(1,128)} %gain_hbm.1, bf16[256,2048]{1,0:T(8,128)(2,1)} %feats_hbm.1, bf16[1,256,2048]{2,1,0:T(8,128)(2,1)} %w_hbm.1), custom_call_target="tpu_custom_call" | custom-call | tf_op jit(solution)/shard_map/pallas_call | solution.py:323
  72.2 1.5 %copy.8 = bf16[16,2048]{1,0:T(8,128)(2,1)} copy(bf16[16,2048]{1,0:T(8,128)(2,1)} %shard_map.64) | data formatting | bytes 131072

commit v4 on v3

--- a/solution.py
+++ b/solution.py
@@ -85,15 +85,15 @@
 def tower_kernel(
     owners, sections, cards,
     seg_hbm, row_hbm, count_hbm, gain_hbm, feats_hbm, w_hbm, out_ref,
-    seg_ref, row_ref, count_ref, gain_ref, feats, weight,
-    sib_out, sib_in, own, cross_out, cross_in, sq_out, sq_in, pooled, xs, done, back, home,
+    seg_ref, row_ref, count_ref, gain_ref, lhs, rhs,
+    sib_out, sib_in, total_ref, cross_out, cross_in, sq_out, sq_in, pooled, xs, done, back, home,
     local_sem, sib_send, sib_recv, cross_send, cross_recv, sq_send, sq_recv,
     x_send, z_send, z_recv, b_send, b_recv, r_send, r_recv,
 ):
     me = lax.axis_index("ingest")
     sec = lax.axis_index("section")
     last = sections - 1
-    width = feats.shape[1]
+    width = feats_hbm.shape[1]
     fb = width // owners
     rows = owners * cards
     slots = row_ref.shape[1]
@@ -114,7 +114,7 @@
         pltpu.make_async_copy(source, to, local_sem.at[n])
         for n, (source, to) in enumerate((
             (seg_hbm, seg_ref), (row_hbm, row_ref), (count_hbm, count_ref),
-            (feats_hbm, feats), (gain_hbm.at[:, cols(me)], gain_ref), (w_hbm.at[0], weight),
+            (feats_hbm, rhs.at[0]), (gain_hbm.at[:, cols(me)], gain_ref), (w_hbm.at[0], rhs.at[1]),
         ))
     ]
     for load in loads:
@@ -122,14 +122,21 @@
 
     barrier = pltpu.get_barrier_semaphore()
 
-    for t in range(1, owners):
-        pl.semaphore_signal(
-            barrier, inc=1, device_id=(lax.rem(me + t, owners), sec), device_id_type=MESH
-        )
-    for t in range(1, sections):
-        pl.semaphore_signal(
-            barrier, inc=1, device_id=(me, lax.rem(sec + t, sections)), device_id_type=MESH
-        )
+    def loop(lo, hi, act):
+        def step(t, carry):
+            act(t)
+            return carry
+
+        lax.fori_loop(lo, hi, step, 0)
+
+    def greet(t):
+        pl.semaphore_signal(barrier, inc=1, device_id=(lax.rem(me + t, owners), sec), device_id_type=MESH)
+
+    def greet_column(t):
+        pl.semaphore_signal(barrier, inc=1, device_id=(me, lax.rem(sec + t, sections)), device_id_type=MESH)
+
+    loop(1, owners, greet)
+    loop(1, sections, greet_column)
     for load in loads[:3]:
         load.wait()
 
@@ -140,13 +147,18 @@
         if j > 0:
             end = end + count_ref[0, j]
         owner = owner + (seg >= end).astype(jnp.int32)
-    row = jnp.zeros_like(seg)
-    for g in range(slots):
-        row = jnp.where(seg == g, row_ref[0, g], row)
+
+    def name_rows(n, row):
+        for g in range(8):
+            row = jnp.where(seg == n * 8 + g, row_ref[0, n * 8 + g], row)
+        return row
+
+    row = lax.fori_loop(0, slots // 8, name_rows, jnp.zeros_like(seg))
     target = owner * cards + row
     ids = lax.broadcasted_iota(jnp.int32, (rows, seg.shape[1]), 0)
-    place = jnp.where(ids == target, 1.0, 0.0).astype(jnp.bfloat16)
-    loads[3].wait()
+    lhs[...] = jnp.where(ids == target, 1.0, 0.0).astype(jnp.bfloat16)
+    for load in loads[3:]:
+        load.wait()
     pl.semaphore_wait(barrier, owners + sections - 2)
 
     def ahead(d):
@@ -171,51 +183,48 @@
             cross_out.at[q, d], cross_in.at[q, c], cross_send.at[q, d], cross_recv.at[q, c], (c * 2 + core, sec)
         ).wait_recv()
 
-    order = list(range(1, chips)) + [0]
-
-    def reduced(q, product):
-        for d in order:
+    def product(q, k):
+        return jnp.dot(
+            lhs[...], rhs[jnp.minimum(q, 1), :, cols(k)], preferred_element_type=jnp.float32
+        )
+
+    def reduced(q):
+        def send_sibling(t):
+            d = lax.rem(t, chips)
             c = ahead(d)
-            sib_out[q, c] = product(c * 2 + 1 - core).astype(jnp.bfloat16)
+            sib_out[q, c] = product(q, c * 2 + 1 - core).astype(jnp.bfloat16)
             sib_copy(q, d).start()
-        for d in order:
+
+        def send_across(t):
+            d = lax.rem(t, chips)
             c = ahead(d)
-            own[d] = product(c * 2 + core)
-        for d in order[:-1]:
+            mine = product(q, c * 2 + core)
             sib_copy(q, d).wait_recv()
-            cross_out[q, d] = (own[d] + sib_in[q, ahead(d)].astype(jnp.float32)).astype(jnp.bfloat16)
-            cross_copy(q, d).start()
-        sib_copy(q, 0).wait_recv()
-        total = own[0] + sib_in[q, chip].astype(jnp.float32)
-        for d in order[:-1]:
+            mine = mine + sib_in[q, c].astype(jnp.float32)
+
+            @pl.when(d > 0)
+            def _():
+                cross_out[q, d] = mine.astype(jnp.bfloat16)
+                cross_copy(q, d).start()
+
+            @pl.when(d == 0)
+            def _():
+                total_ref[...] = mine
+
+        def add(d):
             cross_wait(q, d)
-            total = total + cross_in[q, behind(d)].astype(jnp.float32)
-        return total
+            total_ref[...] += cross_in[q, behind(d)].astype(jnp.float32)
+
+        loop(1, chips + 1, send_sibling)
+        loop(1, chips + 1, send_across)
+        loop(1, chips, add)
 
     def reduced_sends(q):
-        for d in order:
-            sib_copy(q, d).wait_send()
-        for d in order[:-1]:
-            cross_copy(q, d).wait_send()
-
-    x0 = reduced(
-        sections, lambda k: jnp.dot(place, feats[:, cols(k)], preferred_element_type=jnp.float32)
-    ).astype(jnp.bfloat16)
+        loop(0, chips, lambda d: sib_copy(q, d).wait_send())
+        loop(1, chips, lambda d: cross_copy(q, d).wait_send())
 
     def entry_copy():
         return remote(pooled, xs.at[sec], x_send.at[0], z_recv.at[sec], (me, 0))
-
-    @pl.when(sec == 0)
-    def _():
-        xs[0] = x0
-
-    @pl.when(sec > 0)
-    def _():
-        pooled[...] = x0
-        entry_copy().start()
-
-    loads[4].wait()
-    loads[5].wait()
 
     def sq_copy(m, t):
         to = lax.rem(me + t, owners)
@@ -224,7 +233,6 @@
     def sq_wait(m, t):
         frm = lax.rem(me + owners - t, owners)
         remote(sq_out.at[m], sq_in.at[m, frm], sq_send.at[m, t], sq_recv.at[m, frm], (frm, sec)).wait_recv()
-        return sq_in[m, frm]
 
     def next_copy(m):
         return remote(done.at[m], xs.at[m], z_send.at[m], z_recv.at[m], (me, sec + 1))
@@ -237,23 +245,25 @@
         piece = back.at[pl.ds(to * cards, cards)]
         return remote(piece, home.at[me], r_send.at[t], r_recv.at[me], (to, sec))
 
-    def each(m, carry):
+    def enter(m):
         @pl.when(sec + m > 0)
         def _():
             remote(xs.at[m], xs.at[m], z_send.at[m], z_recv.at[m], (me, 0)).wait_recv()
 
         u = xs[m].astype(jnp.float32)
-        h = (u * gain_ref[...]).astype(jnp.bfloat16)
+        lhs[...] = (u * gain_ref[...]).astype(jnp.bfloat16)
         sq = jnp.broadcast_to(jnp.sum(u * u, axis=1, keepdims=True), (rows, LANES))
         sq_out[m] = jnp.transpose(sq)[:8]
-        for t in range(1, owners):
-            sq_copy(m, t).start()
-        y = reduced(m, lambda k: jnp.dot(h, weight[:, cols(k)], preferred_element_type=jnp.float32))
-        sq = sq_out[m]
-        for t in range(1, owners):
-            sq = sq + sq_wait(m, t)
+        loop(1, owners, lambda t: sq_copy(m, t).start())
+
+    def leave(m):
+        def add_sq(t, sq):
+            sq_wait(m, t)
+            return sq + sq_in[m, lax.rem(me + owners - t, owners)]
+
+        sq = lax.fori_loop(1, owners, add_sq, sq_out[m])
         scale = lax.rsqrt(sq / width + 1e-05)
-        y = y * jnp.transpose(scale)[:, :1]
+        y = total_ref[...] * jnp.transpose(scale)[:, :1]
         u = xs[m].astype(jnp.float32)
         done[m] = (u + y / (1.0 + jnp.exp(-y))).astype(jnp.bfloat16)
 
@@ -265,9 +275,32 @@
         def _():
             back_copy(m).start()
 
-        return carry
-
-    lax.fori_loop(0, sections, each, 0)
+    def leave_pool():
+        @pl.when(sec == 0)
+        def _():
+            xs[0] = total_ref[...].astype(jnp.bfloat16)
+
+        @pl.when(sec > 0)
+        def _():
+            pooled[...] = total_ref[...].astype(jnp.bfloat16)
+            entry_copy().start()
+
+    def each(q):
+        @pl.when(q > 0)
+        def _():
+            enter(q - 1)
+
+        reduced(q)
+
+        @pl.when(q > 0)
+        def _():
+            leave(q - 1)
+
+        @pl.when(q == 0)
+        def _():
+            leave_pool()
+
+    loop(0, sections + 1, each)
 
     @pl.when(sec == last)
     def _():
@@ -277,25 +310,24 @@
     def _():
         remote(back, back, b_send.at[0], b_recv.at[0], (me, last)).wait_recv()
 
-    for t in range(1, owners):
-        home_copy(t).start()
+    loop(1, owners, lambda t: home_copy(t).start())
     out_ref[:, cols(me)] = back[pl.ds(me * cards, cards)]
-    for t in range(1, owners):
+
+    def gather(t):
         frm = lax.rem(me + owners - t, owners)
         remote(home.at[frm], home.at[frm], r_send.at[t], r_recv.at[frm], (frm, sec)).wait_recv()
         out_ref[:, cols(frm)] = home[frm]
-        home_copy(t).wait_send()
-
-    reduced_sends(sections)
+
+    loop(1, owners, gather)
+    loop(1, owners, lambda t: home_copy(t).wait_send())
+    loop(0, sections + 1, reduced_sends)
 
     @pl.when(sec > 0)
     def _():
         entry_copy().wait_send()
 
-    def finish(m, carry):
-        reduced_sends(m)
-        for t in range(1, owners):
-            sq_copy(m, t).wait_send()
+    def finish(m):
+        loop(1, owners, lambda t: sq_copy(m, t).wait_send())
 
         @pl.when(sec < last)
         def _():
@@ -305,9 +337,7 @@
         def _():
             back_copy(m).wait_send()
 
-        return carry
-
-    lax.fori_loop(0, sections, finish, 0)
+    loop(0, sections, finish)
 
 
 def kernel_body(owners, sections, txn_feats, txn_seg, seg_row, send_counts, gains, tower_w):
@@ -330,11 +360,11 @@
             pltpu.SMEM(seg_row.shape, jnp.int32),
             pltpu.SMEM(send_counts.shape, jnp.int32),
             pltpu.VMEM((1, fb), jnp.float32),
-            pltpu.VMEM(txn_feats.shape, bf),
-            pltpu.VMEM((fb, width), bf),
+            pltpu.VMEM((rows, fb), bf),
+            pltpu.VMEM((2, fb, width), bf),
             pltpu.VMEM((stages, chips, rows, fb), bf),
             pltpu.VMEM((stages, chips, rows, fb), bf),
-            pltpu.VMEM((chips, rows, fb), jnp.float32),
+            pltpu.VMEM((rows, fb), jnp.float32),
             pltpu.VMEM((stages, chips, rows, fb), bf),
             pltpu.VMEM((stages, chips, rows, fb), bf),
             pltpu.VMEM((sections, 8, rows), jnp.float32),
@@ -379,7 +409,9 @@
 
     def body(txn_feats, txn_seg, seg_row, send_counts, gains, tower_w):
         args = (txn_feats, txn_seg, seg_row, send_counts, gains, tower_w)
-        if owners % 2 == 0 and owners * CARD_DEV % LANES == 0 and txn_feats.shape[1] % (owners * LANES) == 0:
+        depth, width = txn_feats.shape
+        whole = owners * CARD_DEV % LANES == 0 and width % (owners * LANES) == 0
+        if owners % 2 == 0 and whole and depth == width // owners and seg_row.shape[1] % 8 == 0:
             return kernel_body(owners, sections, *args)
         return plain_body(*args)
 

time: 73.8 us -> 76.2 us (1.033)
  Pallas kernels: 72.2 us -> 74.5 us
    pallas_call x1, Pallas kernels: 72.2 us -> 74.5 us  [kernel_body(): pl.pallas_call(functools.partial(tower_kernel, owners, sections, cards),...]
where the time goes in v4:
time: 76.2 us; the launch traced here: 76 us
  Pallas kernels  74.5 us (98%)
  local copies, waits for them, and re-layouts  1.47 us (2%)
    pallas_call x1, Pallas kernels, kernel_body(): pl.pallas_call(functools.partial(tower_kernel, owners, sections, cards),...  74.5 us

profile of v4, /device:TPU:25, one launch (start us, length us, event | category | flops | bytes accessed | tf_op | source)
XLA Modules:
  0.0 76.0 jit_solution(14183197877915142344)
XLA Ops:
  0.0 74.5 %shard_map.64 = bf16[16,2048]{1,0:T(8,128)(2,1)} custom-call(s32[1,256]{1,0:T(1,128)} %seg_hbm.1, s32[1,64]{1,0:T(1,128)} %row_hbm.1, s32[1,8]{1,0:T(1,128)} %count_hbm.1, f32[1,2048]{1,0:T(1,128)} %gain_hbm.1, bf16[256,2048]{1,0:T(8,128)(2,1)} %feats_hbm.1, bf16[1,256,2048]{2,1,0:T(8,128)(2,1)} %w_hbm.1), custom_call_target="tpu_custom_call" | custom-call | tf_op jit(solution)/shard_map/pallas_call | solution.py:353
  74.5 1.5 %copy.8 = bf16[16,2048]{1,0:T(8,128)(2,1)} copy(bf16[16,2048]{1,0:T(8,128)(2,1)} %shard_map.64) | data formatting | bytes 131072

commit v5 on v3

--- a/solution.py
+++ b/solution.py
@@ -86,7 +86,7 @@
     owners, sections, cards,
     seg_hbm, row_hbm, count_hbm, gain_hbm, feats_hbm, w_hbm, out_ref,
     seg_ref, row_ref, count_ref, gain_ref, feats, weight,
-    sib_out, sib_in, own, cross_out, cross_in, sq_out, sq_in, pooled, xs, done, back, home,
+    sib_out, sib_in, own, total_ref, cross_out, cross_in, sq_out, sq_in, pooled, xs, done, back, home,
     local_sem, sib_send, sib_recv, cross_send, cross_recv, sq_send, sq_recv,
     x_send, z_send, z_recv, b_send, b_recv, r_send, r_recv,
 ):
@@ -173,20 +173,24 @@
 
     order = list(range(1, chips)) + [0]
 
-    def reduced(q, product):
+    def share(q, product):
         for d in order:
             c = ahead(d)
             sib_out[q, c] = product(c * 2 + 1 - core).astype(jnp.bfloat16)
             sib_copy(q, d).start()
         for d in order:
-            c = ahead(d)
-            own[d] = product(c * 2 + core)
+            own[d] = product(ahead(d) * 2 + core)
+
+    def across(q):
         for d in order[:-1]:
             sib_copy(q, d).wait_recv()
             cross_out[q, d] = (own[d] + sib_in[q, ahead(d)].astype(jnp.float32)).astype(jnp.bfloat16)
             cross_copy(q, d).start()
         sib_copy(q, 0).wait_recv()
-        total = own[0] + sib_in[q, chip].astype(jnp.float32)
+        total_ref[...] = own[0] + sib_in[q, chip].astype(jnp.float32)
+
+    def collect(q):
+        total = total_ref[...]
         for d in order[:-1]:
             cross_wait(q, d)
             total = total + cross_in[q, behind(d)].astype(jnp.float32)
@@ -198,9 +202,9 @@
         for d in order[:-1]:
             cross_copy(q, d).wait_send()
 
-    x0 = reduced(
-        sections, lambda k: jnp.dot(place, feats[:, cols(k)], preferred_element_type=jnp.float32)
-    ).astype(jnp.bfloat16)
+    share(sections, lambda k: jnp.dot(place, feats[:, cols(k)], preferred_element_type=jnp.float32))
+    across(sections)
+    x0 = collect(sections).astype(jnp.bfloat16)
 
     def entry_copy():
         return remote(pooled, xs.at[sec], x_send.at[0], z_recv.at[sec], (me, 0))
@@ -237,7 +241,7 @@
         piece = back.at[pl.ds(to * cards, cards)]
         return remote(piece, home.at[me], r_send.at[t], r_recv.at[me], (to, sec))
 
-    def each(m, carry):
+    def enter(m):
         @pl.when(sec + m > 0)
         def _():
             remote(xs.at[m], xs.at[m], z_send.at[m], z_recv.at[m], (me, 0)).wait_recv()
@@ -248,7 +252,10 @@
         sq_out[m] = jnp.transpose(sq)[:8]
         for t in range(1, owners):
             sq_copy(m, t).start()
-        y = reduced(m, lambda k: jnp.dot(h, weight[:, cols(k)], preferred_element_type=jnp.float32))
+        share(m, lambda k: jnp.dot(h, weight[:, cols(k)], preferred_element_type=jnp.float32))
+
+    def leave(m):
+        y = collect(m)
         sq = sq_out[m]
         for t in range(1, owners):
             sq = sq + sq_wait(m, t)
@@ -265,9 +272,22 @@
         def _():
             back_copy(m).start()
 
+    def each(m, carry):
+        @pl.when(m < sections)
+        def _():
+            enter(m)
+
+        @pl.when(m > 0)
+        def _():
+            leave(m - 1)
+
+        @pl.when(m < sections)
+        def _():
+            across(m)
+
         return carry
 
-    lax.fori_loop(0, sections, each, 0)
+    lax.fori_loop(0, sections + 1, each, 0)
 
     @pl.when(sec == last)
     def _():
@@ -335,6 +355,7 @@
             pltpu.VMEM((stages, chips, rows, fb), bf),
             pltpu.VMEM((stages, chips, rows, fb), bf),
             pltpu.VMEM((chips, rows, fb), jnp.float32),
+            pltpu.VMEM((rows, fb), jnp.float32),
             pltpu.VMEM((stages, chips, rows, fb), bf),
             pltpu.VMEM((stages, chips, rows, fb), bf),
             pltpu.VMEM((sections, 8, rows), jnp.float32),

time: 73.8 us -> 69.3 us (0.939)
  Pallas kernels: 72.2 us -> 67.6 us
    pallas_call x1, Pallas kernels: 72.2 us -> 67.6 us  [kernel_body(): pl.pallas_call(functools.partial(tower_kernel, owners, sections, cards),...]
where the time goes in v5:
time: 69.3 us; the launch traced here: 69.1 us
  Pallas kernels  67.6 us (98%)
  local copies, waits for them, and re-layouts  1.47 us (2%)
    pallas_call x1, Pallas kernels, kernel_body(): pl.pallas_call(functools.partial(tower_kernel, owners, sections, cards),...  67.6 us
    unnamed x1, local copies, waits for them, and re-layouts  1.47 us

profile of v5, /device:TPU:25, one launch (start us, length us, event | category | flops | bytes accessed | tf_op | source)
XLA Modules:
  0.0 69.1 jit_solution(7483429963250375874)
XLA Ops:
  0.0 67.6 %shard_map.64 = bf16[16,2048]{1,0:T(8,128)(2,1)} custom-call(s32[1,256]{1,0:T(1,128)} %seg_hbm.1, s32[1,64]{1,0:T(1,128)} %row_hbm.1, s32[1,8]{1,0:T(1,128)} %count_hbm.1, f32[1,2048]{1,0:T(1,128)} %gain_hbm.1, bf16[256,2048]{1,0:T(8,128)(2,1)} %feats_hbm.1, bf16[1,256,2048]{2,1,0:T(8,128)(2,1)} %w_hbm.1), custom_call_target="tpu_custom_call" | custom-call | tf_op jit(solution)/shard_map/pallas_call | solution.py:343
  67.6 1.5 %copy.8 = bf16[16,2048]{1,0:T(8,128)(2,1)} copy(bf16[16,2048]{1,0:T(8,128)(2,1)} %shard_map.64) | data formatting | bytes 131072

commit v6 on v5

--- a/solution.py
+++ b/solution.py
@@ -147,7 +147,6 @@
     ids = lax.broadcasted_iota(jnp.int32, (rows, seg.shape[1]), 0)
     place = jnp.where(ids == target, 1.0, 0.0).astype(jnp.bfloat16)
     loads[3].wait()
-    pl.semaphore_wait(barrier, owners + sections - 2)
 
     def ahead(d):
         return lax.rem(chip + d, chips)
@@ -178,6 +177,8 @@
             c = ahead(d)
             sib_out[q, c] = product(c * 2 + 1 - core).astype(jnp.bfloat16)
             sib_copy(q, d).start()
+
+    def keep(product):
         for d in order:
             own[d] = product(ahead(d) * 2 + core)
 
@@ -202,7 +203,12 @@
         for d in order[:-1]:
             cross_copy(q, d).wait_send()
 
-    share(sections, lambda k: jnp.dot(place, feats[:, cols(k)], preferred_element_type=jnp.float32))
+    def pool(k):
+        return jnp.dot(place, feats[:, cols(k)], preferred_element_type=jnp.float32)
+
+    keep(pool)
+    pl.semaphore_wait(barrier, owners + sections - 2)
+    share(sections, pool)
     across(sections)
     x0 = collect(sections).astype(jnp.bfloat16)
 
@@ -248,11 +254,16 @@
 
         u = xs[m].astype(jnp.float32)
         h = (u * gain_ref[...]).astype(jnp.bfloat16)
+
+        def layer(k):
+            return jnp.dot(h, weight[:, cols(k)], preferred_element_type=jnp.float32)
+
+        share(m, layer)
         sq = jnp.broadcast_to(jnp.sum(u * u, axis=1, keepdims=True), (rows, LANES))
         sq_out[m] = jnp.transpose(sq)[:8]
         for t in range(1, owners):
             sq_copy(m, t).start()
-        share(m, lambda k: jnp.dot(h, weight[:, cols(k)], preferred_element_type=jnp.float32))
+        keep(layer)
 
     def leave(m):
         y = collect(m)

time: 69.3 us -> 69.5 us (level)
  no operation moved by 1% of the time
where the time goes in v6:
time: 69.5 us; the launch traced here: 69.3 us
  Pallas kernels  67.8 us (98%)
  local copies, waits for them, and re-layouts  1.47 us (2%)
    pallas_call x1, Pallas kernels, kernel_body(): pl.pallas_call(functools.partial(tower_kernel, owners, sections, cards),...  67.8 us
    unnamed x1, local copies, waits for them, and re-layouts  1.47 us

profile of v6, /device:TPU:25, one launch (start us, length us, event | category | flops | bytes accessed | tf_op | source)
XLA Modules:
  0.0 69.3 jit_solution(2431663261627610481)
XLA Ops:
  0.0 67.8 %shard_map.64 = bf16[16,2048]{1,0:T(8,128)(2,1)} custom-call(s32[1,256]{1,0:T(1,128)} %seg_hbm.1, s32[1,64]{1,0:T(1,128)} %row_hbm.1, s32[1,8]{1,0:T(1,128)} %count_hbm.1, f32[1,2048]{1,0:T(1,128)} %gain_hbm.1, bf16[256,2048]{1,0:T(8,128)(2,1)} %feats_hbm.1, bf16[1,256,2048]{2,1,0:T(8,128)(2,1)} %w_hbm.1), custom_call_target="tpu_custom_call" | custom-call | tf_op jit(solution)/shard_map/pallas_call | solution.py:354
  67.8 1.5 %copy.8 = bf16[16,2048]{1,0:T(8,128)(2,1)} copy(bf16[16,2048]{1,0:T(8,128)(2,1)} %shard_map.64) | data formatting | bytes 131072
